TPU v7x, 256 devices: a whole 4x4x8 slice. The times are simulated.
256 devices in a mesh: tile: 32 (over z, x), zslab: 8 (over y, core).
Axes of the slice: x: 4, y: 4, z: 8, core: 2. Of those that a mesh axis runs over, the one named last changes fastest.
Arguments:
- band: bfloat16 [32, 4, 128, 64, 512], P('tile', None, 'zslab'), may hold values from -6 to 6
- pairs: int32 [64, 4], replicated, may hold values from 0 to 31, as said below
- extents: int32 [64, 2], replicated, may hold values from 32 to 512, as said below
Outputs:
- maps: float32 [64, 128, 32, 256], P('tile', 'zslab')
Inputs may be any that keep to these rules, and one draw needn't show every extreme that they name: `pairs`: every slot (tile, face) with tile < 32 and face < 4 is named by exactly one pair, and a pair names two different slots. `extents`: column 0 lies in 32 to 64, column 1 in 256 to 512; some pair has both at their most.
All inputs are finite; a program needn't handle non-finite values.
Results may differ from a plain program's by a relative error of at most 0.012.
The roundings to bfloat16 on the way count: a program that leaves them out, or rounds other values in their place, can miss the bound.
Values may be sent and summed in bfloat16 or wider, within the bound.
A program may use at most 64 MiB of HBM per device.

v0:
```python
import math
import jax
import jax.numpy as jnp
from jax import lax
from jax.sharding import PartitionSpec as P

GX = 32
GY = 256
GZ = 128
FACES = 4


def dft_tables(length):
    indices = jnp.arange(length, dtype=jnp.int32)
    modular = indices[:, None] * indices[None, :] % length
    angles = modular.astype(jnp.float32) * (2.0 * math.pi / length)
    factor = 1.0 / math.sqrt(length)
    return (
        (jnp.cos(angles) * factor).astype(jnp.bfloat16),
        (jnp.sin(angles) * factor).astype(jnp.bfloat16),
    )


def product(form, left, right):
    return jnp.einsum(form, left, right, preferred_element_type=jnp.float32)


def reduce_resolution(image_volume, crop_bounds):
    row_mask = (
        jnp.arange(image_volume.shape[2], dtype=jnp.int32)[None, :] < crop_bounds[:, 0:1]
    ).astype(jnp.bfloat16)
    col_mask = (
        jnp.arange(image_volume.shape[3], dtype=jnp.int32)[None, :] < crop_bounds[:, 1:2]
    ).astype(jnp.bfloat16)
    masked = image_volume * row_mask[:, None, :, None] * col_mask[:, None, None, :]
    raw_cols = jnp.arange(image_volume.shape[3], dtype=jnp.int32)
    pooled_cols = jnp.arange(GY, dtype=jnp.int32)
    pooling = jnp.where(raw_cols[:, None] // 2 == pooled_cols[None, :], 0.5, 0.0).astype(
        jnp.bfloat16
    )
    along_pooled = product("szxy,yk->szxk", masked, pooling)
    shaped = along_pooled.reshape(image_volume.shape[0], image_volume.shape[1], GX, 2, GY)
    return (shaped[:, :, :, 0, :] + shaped[:, :, :, 1, :]).astype(jnp.bfloat16)


def cross_phase(owner_re, owner_im, pairs, tiles_here):
    first_dev = pairs[:, 0] // tiles_here
    first_pos = pairs[:, 0] % tiles_here * FACES + pairs[:, 1]
    second_tile_device = pairs[:, 2] // tiles_here
    second_pos = pairs[:, 2] % tiles_here * FACES + pairs[:, 3]
    first_re = owner_re[first_dev, :, first_pos].astype(jnp.float32)
    first_im = owner_im[first_dev, :, first_pos].astype(jnp.float32)
    second_re = owner_re[second_tile_device, :, second_pos].astype(jnp.float32)
    second_im = owner_im[second_tile_device, :, second_pos].astype(jnp.float32)
    cross_re = first_re * second_re + first_im * second_im
    cross_im = first_im * second_re - first_re * second_im
    scaled = jnp.sqrt(cross_re * cross_re + cross_im * cross_im + 1.0)
    return ((cross_re / scaled).astype(jnp.bfloat16), (cross_im / scaled).astype(jnp.bfloat16))


def inverse_z(phase_real_part, phase_im, tables_z):
    w_re = (
        product("pmjk,mz->pzjk", phase_real_part, tables_z[0])
        - product("pmjk,mz->pzjk", phase_im, tables_z[1])
    ).astype(jnp.bfloat16)
    w_im = (
        product("pmjk,mz->pzjk", phase_im, tables_z[0])
        + product("pmjk,mz->pzjk", phase_real_part, tables_z[1])
    ).astype(jnp.bfloat16)
    return (w_re, w_im)


def inverse_x(w_re, w_im, tables_x):
    v_re = (
        product("pzjk,jx->pzxk", w_re, tables_x[0]) - product("pzjk,jx->pzxk", w_im, tables_x[1])
    ).astype(jnp.bfloat16)
    v_im = (
        product("pzjk,jx->pzxk", w_im, tables_x[0]) + product("pzjk,jx->pzxk", w_re, tables_x[1])
    ).astype(jnp.bfloat16)
    return (v_re, v_im)


def shards(band, pairs, extents):
    tables_x = dft_tables(GX)
    tables_y = dft_tables(GY)
    tables_z = dft_tables(GZ)
    tiles_here = band.shape[0]
    slots = tiles_here * FACES
    zrows = band.shape[2]
    tile_pos = lax.axis_index("tile")
    global_slot = tile_pos * slots + jnp.arange(slots, dtype=jnp.int32)
    first_slot = pairs[:, 0] * FACES + pairs[:, 1]
    second_slot = pairs[:, 2] * FACES + pairs[:, 3]
    matches = (
        (first_slot[None, :] == global_slot[:, None])
        | (second_slot[None, :] == global_slot[:, None])
    ).astype(jnp.int32)
    crop_bounds = jnp.sum(matches[:, :, None] * extents[None, :, :], axis=1)
    image_volume = band.reshape(slots, zrows, 2 * GX, 2 * GY)
    reduced_volume = reduce_resolution(image_volume, crop_bounds)
    y_re = product("szxy,yk->szxk", reduced_volume, tables_y[0]).astype(jnp.bfloat16)
    y_im = (-product("szxy,yk->szxk", reduced_volume, tables_y[1])).astype(jnp.bfloat16)
    x_re = (
        product("szxk,xj->szjk", y_re, tables_x[0]) + product("szxk,xj->szjk", y_im, tables_x[1])
    ).astype(jnp.bfloat16)
    x_im = (
        product("szxk,xj->szjk", y_im, tables_x[0]) - product("szxk,xj->szjk", y_re, tables_x[1])
    ).astype(jnp.bfloat16)
    kx_part = GX // lax.axis_size("zslab")
    re_in = lax.all_to_all(x_re, "zslab", split_axis=2, concat_axis=1, tiled=True)
    im_in = lax.all_to_all(x_im, "zslab", split_axis=2, concat_axis=1, tiled=True)
    out_re = (
        product("szjk,zm->msjk", re_in, tables_z[0]) + product("szjk,zm->msjk", im_in, tables_z[1])
    ).astype(jnp.bfloat16)
    out_im = (
        product("szjk,zm->msjk", im_in, tables_z[0]) - product("szjk,zm->msjk", re_in, tables_z[1])
    ).astype(jnp.bfloat16)
    tile_count = lax.axis_size("tile")
    kz_part = GZ // tile_count
    spectra = (
        lax.all_to_all(out_re, "tile", split_axis=0, concat_axis=0, tiled=True),
        lax.all_to_all(out_im, "tile", split_axis=0, concat_axis=0, tiled=True),
    )
    owner_re = spectra[0].reshape(tile_count, kz_part, slots, kx_part, GY)
    owner_im = spectra[1].reshape(tile_count, kz_part, slots, kx_part, GY)
    phase_real_part, phase_im = cross_phase(owner_re, owner_im, pairs, tiles_here)
    returned = (
        lax.all_to_all(phase_real_part, "tile", split_axis=0, concat_axis=1, tiled=True),
        lax.all_to_all(phase_im, "tile", split_axis=0, concat_axis=1, tiled=True),
    )
    w_re, w_im = inverse_z(returned[0], returned[1], tables_z)
    v_re, v_im = inverse_x(
        lax.all_to_all(w_re, "zslab", split_axis=1, concat_axis=2, tiled=True),
        lax.all_to_all(w_im, "zslab", split_axis=1, concat_axis=2, tiled=True),
        tables_x,
    )
    return product("pzxk,ky->pzxy", v_re, tables_y[0]) - product("pzxk,ky->pzxy", v_im, tables_y[1])


def solution(mesh):
    placed = (P("tile", None, "zslab", None, None), P(), P())
    return jax.shard_map(
        shards,
        mesh=mesh,
        in_specs=placed,
        out_specs=P("tile", "zslab", None, None),
        check_vma=False,
    )
```

profile of v0, /device:TPU:1, one launch (start us, length us, event | category | flops | bytes accessed | tf_op | source)
XLA Modules:
  0.0 219.9 jit_solution(18191489263805402491)
XLA Ops:
  0.0 0.8 fusion.100
  0.9 0.1 or_convert_fusion
  0.9 0.8 multiply_reduce_fusion
  1.8 0.1 fusion.85
  1.8 7.2 %reshape.185 = bf16[4,16,32,2,512]{4,3,2,1,0:T(2,128)(2,1)} reshape(bf16[1,4,16,64,512]{4,3,2,1,0:T(8,128)(2,1)} %param.3) | data formatting | bytes 8388608 | tf_op jit(solution)/shard_map/reshape | solution.py:99
  9.1 0.1 compare_convert_fusion
  9.1 3.6 %fusion.1 = f32[4,16,32,2,256]{4,2,3,1,0:T(8,128)S(1)} fusion(bf16[4,16,32,2,512]{4,3,2,1,0:T(2,128)(2,1)} %reshape.185, bf16[4,512]{1,0:T(4,128)(2,1)S(1)} %fusion.85, bf16[4,32,2]{1,2,0:T(2,128)(2,1)S(1)} %compare_convert_fusion, s32[512]{0:T(512)S(1)} %add_select_fusion.3), kind=kOutput, calls=%fused_computation.6 | convolution fusion | flops 1078329344 | bytes 8395264 | tf_op jit(solution)/shard_map/szxy,yk->szxk/dot_general | solution.py:25
  12.7 0.4 fusion.19
  13.1 1.4 negate_convert_fusion
  14.5 1.4 convolution_convert_fusion
  15.8 0.5 fusion.83
  16.3 0.5 fusion.6
  16.9 1.6 copy.118
  18.4 6.7 %all-to-all-start = ((bf16[4,16,32,256]{3,1,0,2:T(8,128)(2,1)}), bf16[4,16,32,256]{3,1,0,2:T(8,128)(2,1)S(1)}, u32[]{:S(2)}, u32[]{:S(2)}) async-start(bf16[4,16,32,256]{3,1,0,2:T(8,128)(2,1)} %copy.118), calls=%async_computation | async-start | bytes 2097152 | tf_op jit(solution)/shard_map/all_to_all | solution.py:110
  25.1 0.5 fusion.81
  25.6 0.5 fusion.7
  26.1 1.6 copy.120
  27.7 12.6 %all-to-all-done = bf16[4,16,32,256]{3,1,0,2:T(8,128)(2,1)S(1)} async-done(((bf16[4,16,32,256]{3,1,0,2:T(8,128)(2,1)}), bf16[4,16,32,256]{3,1,0,2:T(8,128)(2,1)S(1)}, u32[]{:S(2)}, u32[]{:S(2)}) %all-to-all-start) | async-done | bytes 1048608 | tf_op jit(solution)/shard_map/all_to_all | solution.py:110
  40.2 4.3 %all-to-all-start.1 = ((bf16[4,16,32,256]{3,1,0,2:T(8,128)(2,1)}), bf16[4,16,32,256]{3,1,0,2:T(8,128)(2,1)S(1)}, u32[]{:S(2)}, u32[]{:S(2)}) async-start(bf16[4,16,32,256]{3,1,0,2:T(8,128)(2,1)} %copy.120), calls=%async_computation.1 | async-start | bytes 2097152 | tf_op jit(solution)/shard_map/all_to_all | solution.py:111
  44.6 0.1 copy.119
  44.7 15.0 %all-to-all-done.1 = bf16[4,16,32,256]{3,1,0,2:T(8,128)(2,1)S(1)} async-done(((bf16[4,16,32,256]{3,1,0,2:T(8,128)(2,1)}), bf16[4,16,32,256]{3,1,0,2:T(8,128)(2,1)S(1)}, u32[]{:S(2)}, u32[]{:S(2)}) %all-to-all-start.1) | async-done | bytes 1048608 | tf_op jit(solution)/shard_map/all_to_all | solution.py:111
  59.7 1.0 copy-done
  60.7 1.3 copy.121
  62.0 0.6 fusion.61
  62.6 0.6 subtract_convert_fusion
  63.3 1.8 copy.125
  65.1 10.5 %all-to-all-start.3 = ((bf16[128,4,4,256]{3,2,1,0:T(4,128)(2,1)}), bf16[128,4,4,256]{3,2,1,0:T(4,128)(2,1)S(1)}, u32[]{:S(2)}, u32[]{:S(2)}) async-start(bf16[128,4,4,256]{3,2,1,0:T(4,128)(2,1)} %copy.125), calls=%async_computation.3 | async-start | bytes 2097152 | tf_op jit(solution)/shard_map/all_to_all | solution.py:122
  75.6 0.6 fusion.63
  76.2 0.7 add_convert_fusion
  76.9 1.8 copy.122
  78.7 22.7 %all-to-all-done.3 = bf16[128,4,4,256]{3,2,1,0:T(4,128)(2,1)S(1)} async-done(((bf16[128,4,4,256]{3,2,1,0:T(4,128)(2,1)}), bf16[128,4,4,256]{3,2,1,0:T(4,128)(2,1)S(1)}, u32[]{:S(2)}, u32[]{:S(2)}) %all-to-all-start.3) | async-done | bytes 1048608 | tf_op jit(solution)/shard_map/all_to_all | solution.py:122
  101.4 6.3 %all-to-all-start.2 = ((bf16[128,4,4,256]{3,2,1,0:T(4,128)(2,1)}), bf16[128,4,4,256]{3,2,1,0:T(4,128)(2,1)S(1)}, u32[]{:S(2)}, u32[]{:S(2)}) async-start(bf16[128,4,4,256]{3,2,1,0:T(4,128)(2,1)} %copy.122), calls=%async_computation.2 | async-start | bytes 2097152 | tf_op jit(solution)/shard_map/all_to_all | solution.py:121
  107.7 1.1 gather_fusion.3
  108.8 1.1 gather_fusion.2
  109.9 22.5 %all-to-all-done.2 = bf16[128,4,4,256]{3,2,1,0:T(4,128)(2,1)S(1)} async-done(((bf16[128,4,4,256]{3,2,1,0:T(4,128)(2,1)}), bf16[128,4,4,256]{3,2,1,0:T(4,128)(2,1)S(1)}, u32[]{:S(2)}, u32[]{:S(2)}) %all-to-all-start.2) | async-done | bytes 1048608 | tf_op jit(solution)/shard_map/all_to_all | solution.py:121
  132.4 1.1 gather_fusion.1
  133.5 1.1 gather_fusion
  134.6 1.1 divide_convert_fusion
  135.7 1.2 copy.130
  136.9 7.3 %all-to-all-start.5 = ((bf16[64,4,4,256]{3,2,1,0:T(4,128)(2,1)}), bf16[64,4,4,256]{3,2,1,0:T(4,128)(2,1)S(1)}, u32[]{:S(2)}, u32[]{:S(2)}) async-start(bf16[64,4,4,256]{3,2,1,0:T(4,128)(2,1)} %copy.130), calls=%async_computation.5 | async-start | bytes 1048576 | tf_op jit(solution)/shard_map/all_to_all | solution.py:129
  144.3 1.2 copy.128
  145.5 13.2 %all-to-all-done.5 = bf16[64,4,4,256]{3,2,1,0:T(4,128)(2,1)S(1)} async-done(((bf16[64,4,4,256]{3,2,1,0:T(4,128)(2,1)}), bf16[64,4,4,256]{3,2,1,0:T(4,128)(2,1)S(1)}, u32[]{:S(2)}, u32[]{:S(2)}) %all-to-all-start.5) | async-done | bytes 524320 | tf_op jit(solution)/shard_map/all_to_all | solution.py:129
  158.6 5.9 %all-to-all-start.4 = ((bf16[64,4,4,256]{3,2,1,0:T(4,128)(2,1)}), bf16[64,4,4,256]{3,2,1,0:T(4,128)(2,1)S(1)}, u32[]{:S(2)}, u32[]{:S(2)}) async-start(bf16[64,4,4,256]{3,2,1,0:T(4,128)(2,1)} %copy.128), calls=%async_computation.4 | async-start | bytes 1048576 | tf_op jit(solution)/shard_map/all_to_all | solution.py:128
  164.6 0.2 copy.131
  164.8 0.1 all_to_all.101
  164.9 13.5 %all-to-all-done.4 = bf16[64,4,4,256]{3,2,1,0:T(4,128)(2,1)S(1)} async-done(((bf16[64,4,4,256]{3,2,1,0:T(4,128)(2,1)}), bf16[64,4,4,256]{3,2,1,0:T(4,128)(2,1)S(1)}, u32[]{:S(2)}, u32[]{:S(2)}) %all-to-all-start.4) | async-done | bytes 524320 | tf_op jit(solution)/shard_map/all_to_all | solution.py:128
  178.4 0.2 copy.129
  178.6 0.1 all_to_all.97
  178.7 0.5 fusion.59
  179.2 0.5 fusion.16
  179.8 1.2 copy.132
  181.0 8.6 %all-to-all-start.6 = ((bf16[2,128,4,256]{3,2,0,1:T(4,128)(2,1)}), bf16[2,128,4,256]{3,2,0,1:T(4,128)(2,1)S(1)}, u32[]{:S(2)}, u32[]{:S(2)}) async-start(bf16[2,128,4,256]{3,2,0,1:T(4,128)(2,1)} %copy.132), calls=%async_computation.6 | async-start | bytes 1048576 | tf_op jit(solution)/shard_map/all_to_all | solution.py:133
  189.5 0.5 fusion.57
  190.0 0.5 fusion.15
  190.5 1.2 copy.136
  191.7 7.3 %all-to-all-done.6 = bf16[2,128,4,256]{3,2,0,1:T(4,128)(2,1)S(1)} async-done(((bf16[2,128,4,256]{3,2,0,1:T(4,128)(2,1)}), bf16[2,128,4,256]{3,2,0,1:T(4,128)(2,1)S(1)}, u32[]{:S(2)}, u32[]{:S(2)}) %all-to-all-start.6) | async-done | bytes 524320 | tf_op jit(solution)/shard_map/all_to_all | solution.py:133
  199.0 4.3 %all-to-all-start.7 = ((bf16[2,128,4,256]{3,2,0,1:T(4,128)(2,1)}), bf16[2,128,4,256]{3,2,0,1:T(4,128)(2,1)S(1)}, u32[]{:S(2)}, u32[]{:S(2)}) async-start(bf16[2,128,4,256]{3,2,0,1:T(4,128)(2,1)} %copy.136), calls=%async_computation.7 | async-start | bytes 1048576 | tf_op jit(solution)/shard_map/all_to_all | solution.py:134
  203.3 0.1 copy.133
  203.4 9.3 %all-to-all-done.7 = bf16[2,128,4,256]{3,2,0,1:T(4,128)(2,1)S(1)} async-done(((bf16[2,128,4,256]{3,2,0,1:T(4,128)(2,1)}), bf16[2,128,4,256]{3,2,0,1:T(4,128)(2,1)S(1)}, u32[]{:S(2)}, u32[]{:S(2)}) %all-to-all-start.7) | async-done | bytes 524320 | tf_op jit(solution)/shard_map/all_to_all | solution.py:134
  212.8 0.1 copy.137
  212.9 0.4 fusion.20
  213.3 1.4 fusion.26
  214.7 2.7 %fusion.14 = f32[2,16,32,256]{3,2,1,0:T(8,128)S(1)} fusion(f32[32,2,16,256]{3,0,2,1:T(8,128)} %fusion.26, bf16[2,16,32,256]{3,1,2,0:T(8,128)(2,1)S(1)} %bitcast.132), kind=kOutput, calls=%fused_computation.34 | convolution fusion | flops 152584192 | bytes 2621440 | tf_op jit(solution)/shard_map/pzxk,ky->pzxy/dot_general | solution.py:25
  217.4 2.5 %convolution_subtract_fusion = f32[2,16,32,256]{3,2,1,0:T(8,128)} fusion(f32[2,16,32,256]{3,2,1,0:T(8,128)S(1)} %fusion.14, f32[32,2,16,256]{3,0,2,1:T(8,128)S(1)} %fusion.20, bf16[2,16,32,256]{3,1,2,0:T(8,128)(2,1)S(1)} %bitcast.130), kind=kOutput, calls=%fused_computation.19 | convolution fusion | flops 152846336 | bytes 3670016 | tf_op jit(solution)/shard_map/pzxk,ky->pzxy/dot_general | solution.py:25
  (7 shorter events, 0.1 us)
Async XLA Ops:
  18.4 21.8 %all-to-all-start = ((bf16[4,16,32,256]{3,1,0,2:T(8,128)(2,1)}), bf16[4,16,32,256]{3,1,0,2:T(8,128)(2,1)S(1)}, u32[]{:S(2)}, u32[]{:S(2)}) async-start(bf16[4,16,32,256]{3,1,0,2:T(8,128)(2,1)} %copy.118), calls=%async_computation | async-start | bytes 2097152 | tf_op jit(solution)/shard_map/all_to_all | solution.py:110
  40.2 19.5 %all-to-all-start.1 = ((bf16[4,16,32,256]{3,1,0,2:T(8,128)(2,1)}), bf16[4,16,32,256]{3,1,0,2:T(8,128)(2,1)S(1)}, u32[]{:S(2)}, u32[]{:S(2)}) async-start(bf16[4,16,32,256]{3,1,0,2:T(8,128)(2,1)} %copy.120), calls=%async_computation.1 | async-start | bytes 2097152 | tf_op jit(solution)/shard_map/all_to_all | solution.py:111
  59.7 1.0 copy-start
  65.1 36.3 %all-to-all-start.3 = ((bf16[128,4,4,256]{3,2,1,0:T(4,128)(2,1)}), bf16[128,4,4,256]{3,2,1,0:T(4,128)(2,1)S(1)}, u32[]{:S(2)}, u32[]{:S(2)}) async-start(bf16[128,4,4,256]{3,2,1,0:T(4,128)(2,1)} %copy.125), calls=%async_computation.3 | async-start | bytes 2097152 | tf_op jit(solution)/shard_map/all_to_all | solution.py:122
  101.4 31.0 %all-to-all-start.2 = ((bf16[128,4,4,256]{3,2,1,0:T(4,128)(2,1)}), bf16[128,4,4,256]{3,2,1,0:T(4,128)(2,1)S(1)}, u32[]{:S(2)}, u32[]{:S(2)}) async-start(bf16[128,4,4,256]{3,2,1,0:T(4,128)(2,1)} %copy.122), calls=%async_computation.2 | async-start | bytes 2097152 | tf_op jit(solution)/shard_map/all_to_all | solution.py:121
  136.9 21.7 %all-to-all-start.5 = ((bf16[64,4,4,256]{3,2,1,0:T(4,128)(2,1)}), bf16[64,4,4,256]{3,2,1,0:T(4,128)(2,1)S(1)}, u32[]{:S(2)}, u32[]{:S(2)}) async-start(bf16[64,4,4,256]{3,2,1,0:T(4,128)(2,1)} %copy.130), calls=%async_computation.5 | async-start | bytes 1048576 | tf_op jit(solution)/shard_map/all_to_all | solution.py:129
  158.6 19.8 %all-to-all-start.4 = ((bf16[64,4,4,256]{3,2,1,0:T(4,128)(2,1)}), bf16[64,4,4,256]{3,2,1,0:T(4,128)(2,1)S(1)}, u32[]{:S(2)}, u32[]{:S(2)}) async-start(bf16[64,4,4,256]{3,2,1,0:T(4,128)(2,1)} %copy.128), calls=%async_computation.4 | async-start | bytes 1048576 | tf_op jit(solution)/shard_map/all_to_all | solution.py:128
  181.0 18.1 %all-to-all-start.6 = ((bf16[2,128,4,256]{3,2,0,1:T(4,128)(2,1)}), bf16[2,128,4,256]{3,2,0,1:T(4,128)(2,1)S(1)}, u32[]{:S(2)}, u32[]{:S(2)}) async-start(bf16[2,128,4,256]{3,2,0,1:T(4,128)(2,1)} %copy.132), calls=%async_computation.6 | async-start | bytes 1048576 | tf_op jit(solution)/shard_map/all_to_all | solution.py:133
  199.0 13.8 %all-to-all-start.7 = ((bf16[2,128,4,256]{3,2,0,1:T(4,128)(2,1)}), bf16[2,128,4,256]{3,2,0,1:T(4,128)(2,1)S(1)}, u32[]{:S(2)}, u32[]{:S(2)}) async-start(bf16[2,128,4,256]{3,2,0,1:T(4,128)(2,1)} %copy.136), calls=%async_computation.7 | async-start | bytes 1048576 | tf_op jit(solution)/shard_map/all_to_all | solution.py:134
where the time goes:
time: 221 us; the launch traced here: 220 us
  waiting for transfers between devices  116 us (52%)
  starting transfers between devices  53.9 us (24%)
  local copies, waits for them, and re-layouts  26.5 us (12%)
  matrix products  19.9 us (9%)
  other arithmetic  3.4 us (2%)
    all_to_all x1, waiting for transfers between devices, shards(): lax.all_to_all(out_im, 'tile', split_axis=0, concat_axis=0, tiled=True)  22.7 us
    all_to_all x1, waiting for transfers between devices, shards(): lax.all_to_all(out_re, 'tile', split_axis=0, concat_axis=0, tiled=True)  22.5 us
    dot_general x19, matrix products, product(): return jnp.einsum(form, left, right, preferred_element_type=jnp.float32)  19.9 us
    all_to_all x1, waiting for transfers between devices, shards(): lax.all_to_all(x_im, 'zslab', split_axis=2, concat_axis=1, tiled=True)  15 us
    all_to_all x1, waiting for transfers between devices, shards(): lax.all_to_all(phase_real_part, 'tile', split_axis=0, concat_axis=1, tile...  13.5 us
    all_to_all x1, waiting for transfers between devices, shards(): lax.all_to_all(phase_im, 'tile', split_axis=0, concat_axis=1, tiled=True)  13.2 us
    all_to_all x1, waiting for transfers between devices, shards(): lax.all_to_all(x_re, 'zslab', split_axis=2, concat_axis=1, tiled=True)  12.6 us
    all_to_all x1, starting transfers between devices, shards(): lax.all_to_all(out_im, 'tile', split_axis=0, concat_axis=0, tiled=True)  10.5 us
  transfers between devices with their start and end apart: 8, of which 8 were waited for; matrix products, arithmetic and copies ran while one was open for 5% of the time, Pallas kernels for 0%

commit v1 on v0

--- a/solution.py
+++ b/solution.py
@@ -8,6 +8,29 @@
 GY = 256
 GZ = 128
 FACES = 4
+
+
+def in_blocks(x, dim, size):
+    before, after = (x.shape[:dim], x.shape[dim + 1 :])
+    return jnp.moveaxis(x.reshape(*before, size, -1, *after), dim, 0)
+
+
+def joined_along(blocks, dim):
+    shape = list(blocks.shape[1:])
+    shape[dim] *= blocks.shape[0]
+    return jnp.moveaxis(blocks, 0, dim).reshape(shape)
+
+
+def exchange_directly(shard, axis, split_dim, concat_dim):
+    size, position = (lax.axis_size(axis), lax.axis_index(axis))
+    tiles = in_blocks(shard, split_dim, size)
+    result = tiles
+    for step in range(1, size):
+        target, source = ((position + step) % size, (position - step) % size)
+        sent = lax.dynamic_index_in_dim(tiles, target, 0)
+        other = lax.ppermute(sent, axis, [(i, (i + step) % size) for i in range(size)])
+        result = lax.dynamic_update_slice_in_dim(result, other, source, axis=0)
+    return joined_along(result, concat_dim)
 
 
 def dft_tables(length):
@@ -131,7 +154,7 @@
     w_re, w_im = inverse_z(returned[0], returned[1], tables_z)
     v_re, v_im = inverse_x(
         lax.all_to_all(w_re, "zslab", split_axis=1, concat_axis=2, tiled=True),
-        lax.all_to_all(w_im, "zslab", split_axis=1, concat_axis=2, tiled=True),
+        exchange_directly(w_im, "zslab", 1, 2),
         tables_x,
     )
     return product("pzxk,ky->pzxy", v_re, tables_y[0]) - product("pzxk,ky->pzxy", v_im, tables_y[1])

time: 221 us -> 213 us (0.964)
  waiting for transfers between devices: 116 us -> 104 us
  starting transfers between devices: 53.9 us -> 58.6 us
    ppermute x0 -> x7, starting transfers between devices: none -> 14.1 us  [exchange_directly(): lax.ppermute(sent, axis, [(i, (i + step) % size) for i in range(size)])]
    all_to_all x1 -> x0, waiting for transfers between devices: 9.34 us -> none  [shards(): lax.all_to_all(w_im, 'zslab', split_axis=1, concat_axis=2, tiled=True)]
    all_to_all x1, waiting for transfers between devices: 7.29 us -> 0.01 us  [shards(): lax.all_to_all(w_re, 'zslab', split_axis=1, concat_axis=2, tiled=True)]
    ppermute x0 -> x7, waiting for transfers between devices: none -> 6.91 us  [exchange_directly(): lax.ppermute(sent, axis, [(i, (i + step) % size) for i in range(size)])]
    all_to_all x1, starting transfers between devices: 8.56 us -> 3.44 us  [shards(): lax.all_to_all(w_re, 'zslab', split_axis=1, concat_axis=2, tiled=True)]
    all_to_all x1 -> x0, starting transfers between devices: 4.27 us -> none  [shards(): lax.all_to_all(w_im, 'zslab', split_axis=1, concat_axis=2, tiled=True)]
    all_to_all x1, starting transfers between devices: 10.5 us -> 6.34 us  [shards(): lax.all_to_all(out_im, 'tile', split_axis=0, concat_axis=0, tiled=True)]
    all_to_all x1, starting transfers between devices: 6.34 us -> 10.5 us  [shards(): lax.all_to_all(out_re, 'tile', split_axis=0, concat_axis=0, tiled=True)]
  transfers between devices with their start and end apart: 8 -> 14, of which waited for: 8 -> 8; matrix products, arithmetic and copies ran while one was open for 5% -> 6% of each run, Pallas kernels for 0% -> 0%
where the time goes in v1:
time: 213 us; the launch traced here: 212 us
  waiting for transfers between devices  104 us (49%)
  starting transfers between devices  58.6 us (28%)
  local copies, waits for them, and re-layouts  24.6 us (12%)
  matrix products  21.3 us (10%)
  other arithmetic  3.4 us (2%)
    all_to_all x1, waiting for transfers between devices, shards(): lax.all_to_all(out_re, 'tile', split_axis=0, concat_axis=0, tiled=True)  22.7 us
    all_to_all x1, waiting for transfers between devices, shards(): lax.all_to_all(out_im, 'tile', split_axis=0, concat_axis=0, tiled=True)  22.5 us
    dot_general x19, matrix products, product(): return jnp.einsum(form, left, right, preferred_element_type=jnp.float32)  21.3 us
    ppermute x7, starting transfers between devices, exchange_directly(): lax.ppermute(sent, axis, [(i, (i + step) % size) for i in range(size)])  14.1 us
    all_to_all x1, waiting for transfers between devices, shards(): lax.all_to_all(phase_im, 'tile', split_axis=0, concat_axis=1, tiled=True)  13.2 us
    all_to_all x1, waiting for transfers between devices, shards(): lax.all_to_all(x_im, 'zslab', split_axis=2, concat_axis=1, tiled=True)  13 us
    all_to_all x1, waiting for transfers between devices, shards(): lax.all_to_all(phase_real_part, 'tile', split_axis=0, concat_axis=1, tile...  12.7 us
    all_to_all x1, waiting for transfers between devices, shards(): lax.all_to_all(x_re, 'zslab', split_axis=2, concat_axis=1, tiled=True)  12.5 us
  transfers between devices with their start and end apart: 14, of which 8 were waited for; matrix products, arithmetic and copies ran while one was open for 6% of the time, Pallas kernels for 0%

profile of v1, /device:TPU:1, one launch (start us, length us, event | category | flops | bytes accessed | tf_op | source)
XLA Modules:
  0.0 212.0 jit_solution(9550794647022363964)
XLA Ops:
  0.0 0.8 fusion.119
  0.9 0.8 multiply_reduce_fusion
  1.8 7.2 %reshape.198 = bf16[4,16,32,2,512]{4,3,2,1,0:T(2,128)(2,1)} reshape(bf16[1,4,16,64,512]{4,3,2,1,0:T(8,128)(2,1)} %param.3) | data formatting | bytes 8388608 | tf_op jit(solution)/shard_map/reshape | solution.py:122
  9.1 3.6 %fusion.1 = f32[4,16,32,2,256]{4,2,3,1,0:T(8,128)S(1)} fusion(bf16[4,16,32,2,512]{4,3,2,1,0:T(2,128)(2,1)} %reshape.198, bf16[4,512]{1,0:T(4,128)(2,1)S(1)} %fusion.84, bf16[4,32,2]{1,2,0:T(2,128)(2,1)S(1)} %compare_convert_fusion, s32[512]{0:T(512)S(1)} %add_select_fusion.3), kind=kOutput, calls=%fused_computation.6 | convolution fusion | flops 1078329344 | bytes 8395264 | tf_op jit(solution)/shard_map/szxy,yk->szxk/dot_general | solution.py:48
  12.7 0.4 fusion.18
  13.0 1.4 convolution_convert_fusion
  14.4 1.4 negate_convert_fusion
  15.8 0.5 fusion.82
  16.3 0.5 fusion.6
  16.8 1.6 copy.110
  18.4 6.7 %all-to-all-start = ((bf16[4,16,32,256]{3,1,0,2:T(8,128)(2,1)}), bf16[4,16,32,256]{3,1,0,2:T(8,128)(2,1)S(1)}, u32[]{:S(2)}, u32[]{:S(2)}) async-start(bf16[4,16,32,256]{3,1,0,2:T(8,128)(2,1)} %copy.110), calls=%async_computation | async-start | bytes 2097152 | tf_op jit(solution)/shard_map/all_to_all | solution.py:133
  25.1 0.5 fusion.80
  25.6 0.5 fusion.7
  26.1 1.6 copy.112
  27.7 12.5 %all-to-all-done = bf16[4,16,32,256]{3,1,0,2:T(8,128)(2,1)S(1)} async-done(((bf16[4,16,32,256]{3,1,0,2:T(8,128)(2,1)}), bf16[4,16,32,256]{3,1,0,2:T(8,128)(2,1)S(1)}, u32[]{:S(2)}, u32[]{:S(2)}) %all-to-all-start) | async-done | bytes 1048608 | tf_op jit(solution)/shard_map/all_to_all | solution.py:133
  40.2 4.3 %all-to-all-start.1 = ((bf16[4,16,32,256]{3,1,0,2:T(8,128)(2,1)}), bf16[4,16,32,256]{3,1,0,2:T(8,128)(2,1)S(1)}, u32[]{:S(2)}, u32[]{:S(2)}) async-start(bf16[4,16,32,256]{3,1,0,2:T(8,128)(2,1)} %copy.112), calls=%async_computation.1 | async-start | bytes 2097152 | tf_op jit(solution)/shard_map/all_to_all | solution.py:134
  44.6 0.1 copy.111
  44.7 2.0 fusion.62
  46.6 13.0 %all-to-all-done.1 = bf16[4,16,32,256]{3,1,0,2:T(8,128)(2,1)S(1)} async-done(((bf16[4,16,32,256]{3,1,0,2:T(8,128)(2,1)}), bf16[4,16,32,256]{3,1,0,2:T(8,128)(2,1)S(1)}, u32[]{:S(2)}, u32[]{:S(2)}) %all-to-all-start.1) | async-done | bytes 1048608 | tf_op jit(solution)/shard_map/all_to_all | solution.py:134
  59.7 0.1 copy.113
  59.8 1.5 copy-done
  61.3 0.6 add_convert_fusion
  61.9 1.8 copy.114
  63.7 10.5 %all-to-all-start.2 = ((bf16[128,4,4,256]{3,2,1,0:T(4,128)(2,1)}), bf16[128,4,4,256]{3,2,1,0:T(4,128)(2,1)S(1)}, u32[]{:S(2)}, u32[]{:S(2)}) async-start(bf16[128,4,4,256]{3,2,1,0:T(4,128)(2,1)} %copy.114), calls=%async_computation.2 | async-start | bytes 2097152 | tf_op jit(solution)/shard_map/all_to_all | solution.py:144
  74.2 0.6 fusion.60
  74.9 0.7 subtract_convert_fusion
  75.5 1.8 copy.117
  77.3 22.7 %all-to-all-done.2 = bf16[128,4,4,256]{3,2,1,0:T(4,128)(2,1)S(1)} async-done(((bf16[128,4,4,256]{3,2,1,0:T(4,128)(2,1)}), bf16[128,4,4,256]{3,2,1,0:T(4,128)(2,1)S(1)}, u32[]{:S(2)}, u32[]{:S(2)}) %all-to-all-start.2) | async-done | bytes 1048608 | tf_op jit(solution)/shard_map/all_to_all | solution.py:144
  100.0 6.3 %all-to-all-start.3 = ((bf16[128,4,4,256]{3,2,1,0:T(4,128)(2,1)}), bf16[128,4,4,256]{3,2,1,0:T(4,128)(2,1)S(1)}, u32[]{:S(2)}, u32[]{:S(2)}) async-start(bf16[128,4,4,256]{3,2,1,0:T(4,128)(2,1)} %copy.117), calls=%async_computation.3 | async-start | bytes 2097152 | tf_op jit(solution)/shard_map/all_to_all | solution.py:145
  106.3 1.1 gather_fusion.1
  107.5 1.1 gather_fusion
  108.6 22.5 %all-to-all-done.3 = bf16[128,4,4,256]{3,2,1,0:T(4,128)(2,1)S(1)} async-done(((bf16[128,4,4,256]{3,2,1,0:T(4,128)(2,1)}), bf16[128,4,4,256]{3,2,1,0:T(4,128)(2,1)S(1)}, u32[]{:S(2)}, u32[]{:S(2)}) %all-to-all-start.3) | async-done | bytes 1048608 | tf_op jit(solution)/shard_map/all_to_all | solution.py:145
  131.0 1.1 gather_fusion.2
  132.1 1.1 gather_fusion.3
  133.2 1.1 divide_convert_fusion
  134.4 1.2 copy.122
  135.6 7.3 %all-to-all-start.5 = ((bf16[64,4,4,256]{3,2,1,0:T(4,128)(2,1)}), bf16[64,4,4,256]{3,2,1,0:T(4,128)(2,1)S(1)}, u32[]{:S(2)}, u32[]{:S(2)}) async-start(bf16[64,4,4,256]{3,2,1,0:T(4,128)(2,1)} %copy.122), calls=%async_computation.5 | async-start | bytes 1048576 | tf_op jit(solution)/shard_map/all_to_all | solution.py:152
  142.9 1.2 copy.120
  144.1 13.2 %all-to-all-done.5 = bf16[64,4,4,256]{3,2,1,0:T(4,128)(2,1)S(1)} async-done(((bf16[64,4,4,256]{3,2,1,0:T(4,128)(2,1)}), bf16[64,4,4,256]{3,2,1,0:T(4,128)(2,1)S(1)}, u32[]{:S(2)}, u32[]{:S(2)}) %all-to-all-start.5) | async-done | bytes 524320 | tf_op jit(solution)/shard_map/all_to_all | solution.py:152
  157.3 5.9 %all-to-all-start.4 = ((bf16[64,4,4,256]{3,2,1,0:T(4,128)(2,1)}), bf16[64,4,4,256]{3,2,1,0:T(4,128)(2,1)S(1)}, u32[]{:S(2)}, u32[]{:S(2)}) async-start(bf16[64,4,4,256]{3,2,1,0:T(4,128)(2,1)} %copy.120), calls=%async_computation.4 | async-start | bytes 1048576 | tf_op jit(solution)/shard_map/all_to_all | solution.py:151
  163.5 0.2 copy.123
  163.7 0.1 all_to_all.88
  163.8 0.5 fusion.56
  164.3 12.7 %all-to-all-done.4 = bf16[64,4,4,256]{3,2,1,0:T(4,128)(2,1)S(1)} async-done(((bf16[64,4,4,256]{3,2,1,0:T(4,128)(2,1)}), bf16[64,4,4,256]{3,2,1,0:T(4,128)(2,1)S(1)}, u32[]{:S(2)}, u32[]{:S(2)}) %all-to-all-start.4) | async-done | bytes 524320 | tf_op jit(solution)/shard_map/all_to_all | solution.py:151
  177.1 0.2 copy.121
  177.3 0.1 all_to_all.84
  177.4 0.5 fusion.58
  177.9 0.5 fusion.9
  178.5 5.4 %collective-permute-start = (bf16[1,2,16,4,256]{4,2,3,0,1:T(8,128)(2,1)S(1)}, bf16[1,2,16,4,256]{4,2,3,0,1:T(8,128)(2,1)S(1)}, u32[]{:S(2)}, u32[]{:S(2)}) collective-permute-start(bf16[1,2,16,4,256]{4,2,3,0,1:T(8,128)(2,1)S(1)} %get-tuple-element.13), channel_id=1, source_target_pairs={{0,1},{1,2},{2,3},{3,4},{4,5},{5,6},{6,7},{7,0},{8,9},{9,10},{10,1... | collective-permute-start | bytes 196616 | tf_op jit(solution)/shard_map/ppermute | solution.py:31
  183.9 1.1 collective-permute-start.1
  185.0 1.0 collective-permute-start.2
  186.0 1.4 collective-permute-start.3
  187.5 2.6 %collective-permute-start.4 = (bf16[1,2,16,4,256]{4,2,3,0,1:T(8,128)(2,1)S(1)}, bf16[1,2,16,4,256]{4,2,3,0,1:T(8,128)(2,1)S(1)}, u32[]{:S(2)}, u32[]{:S(2)}) collective-permute-start(bf16[1,2,16,4,256]{4,2,3,0,1:T(8,128)(2,1)S(1)} %get-tuple-element.9), channel_id=1, source_target_pairs={{0,5},{1,6},{2,7},{3,0},{4,1},{5,2},{6,3},{7,4},{8,13},{9,14},{10,... | collective-permute-start | bytes 196616 | tf_op jit(solution)/shard_map/ppermute | solution.py:31
  190.1 0.5 fusion.15
  190.6 1.2 copy.124
  191.8 3.4 %all-to-all-start.6 = ((bf16[2,128,4,256]{3,2,0,1:T(4,128)(2,1)}), bf16[2,128,4,256]{3,2,0,1:T(4,128)(2,1)S(1)}, u32[]{:S(2)}, u32[]{:S(2)}) async-start(bf16[2,128,4,256]{3,2,0,1:T(4,128)(2,1)} %copy.124), calls=%async_computation.6 | async-start | bytes 1048576 | tf_op jit(solution)/shard_map/all_to_all | solution.py:156
  195.3 1.9 collective-permute-start.5
  197.1 0.7 collective-permute-start.6
  197.9 6.0 %collective-permute-done.5 = bf16[1,2,16,4,256]{4,2,3,0,1:T(8,128)(2,1)S(1)} collective-permute-done((bf16[1,2,16,4,256]{4,2,3,0,1:T(8,128)(2,1)S(1)}, bf16[1,2,16,4,256]{4,2,3,0,1:T(8,128)(2,1)S(1)}, u32[]{:S(2)}, u32[]{:S(2)}) %collective-permute-start.5) | collective-permute-done | bytes 65568 | tf_op jit(solution)/shard_map/ppermute | solution.py:31
  203.9 0.9 collective-permute-done.6
  205.0 1.4 fusion.25
  206.4 0.4 fusion.23
  206.7 2.7 %fusion.14 = f32[2,16,32,256]{3,2,1,0:T(8,128)S(1)} fusion(f32[32,2,16,256]{3,0,2,1:T(8,128)} %fusion.25, bf16[2,16,32,256]{3,1,2,0:T(8,128)(2,1)S(1)} %bitcast.147), kind=kOutput, calls=%fused_computation.34 | convolution fusion | flops 152584192 | bytes 2621440 | tf_op jit(solution)/shard_map/pzxk,ky->pzxy/dot_general | solution.py:48
  209.5 2.5 %convolution_subtract_fusion = f32[2,16,32,256]{3,2,1,0:T(8,128)} fusion(f32[2,16,32,256]{3,2,1,0:T(8,128)S(1)} %fusion.14, f32[32,2,16,256]{3,0,2,1:T(8,128)S(1)} %fusion.23, bf16[2,16,32,256]{3,1,2,0:T(8,128)(2,1)S(1)} %bitcast.148), kind=kOutput, calls=%fused_computation.19 | convolution fusion | flops 152846336 | bytes 3670016 | tf_op jit(solution)/shard_map/pzxk,ky->pzxy/dot_general | solution.py:48
  (25 shorter events, 0.6 us)
Async XLA Ops:
  18.4 21.8 %all-to-all-start = ((bf16[4,16,32,256]{3,1,0,2:T(8,128)(2,1)}), bf16[4,16,32,256]{3,1,0,2:T(8,128)(2,1)S(1)}, u32[]{:S(2)}, u32[]{:S(2)}) async-start(bf16[4,16,32,256]{3,1,0,2:T(8,128)(2,1)} %copy.110), calls=%async_computation | async-start | bytes 2097152 | tf_op jit(solution)/shard_map/all_to_all | solution.py:133
  40.2 19.5 %all-to-all-start.1 = ((bf16[4,16,32,256]{3,1,0,2:T(8,128)(2,1)}), bf16[4,16,32,256]{3,1,0,2:T(8,128)(2,1)S(1)}, u32[]{:S(2)}, u32[]{:S(2)}) async-start(bf16[4,16,32,256]{3,1,0,2:T(8,128)(2,1)} %copy.112), calls=%async_computation.1 | async-start | bytes 2097152 | tf_op jit(solution)/shard_map/all_to_all | solution.py:134
  59.7 1.6 copy-start
  63.7 36.3 %all-to-all-start.2 = ((bf16[128,4,4,256]{3,2,1,0:T(4,128)(2,1)}), bf16[128,4,4,256]{3,2,1,0:T(4,128)(2,1)S(1)}, u32[]{:S(2)}, u32[]{:S(2)}) async-start(bf16[128,4,4,256]{3,2,1,0:T(4,128)(2,1)} %copy.114), calls=%async_computation.2 | async-start | bytes 2097152 | tf_op jit(solution)/shard_map/all_to_all | solution.py:144
  100.0 31.0 %all-to-all-start.3 = ((bf16[128,4,4,256]{3,2,1,0:T(4,128)(2,1)}), bf16[128,4,4,256]{3,2,1,0:T(4,128)(2,1)S(1)}, u32[]{:S(2)}, u32[]{:S(2)}) async-start(bf16[128,4,4,256]{3,2,1,0:T(4,128)(2,1)} %copy.117), calls=%async_computation.3 | async-start | bytes 2097152 | tf_op jit(solution)/shard_map/all_to_all | solution.py:145
  135.6 21.7 %all-to-all-start.5 = ((bf16[64,4,4,256]{3,2,1,0:T(4,128)(2,1)}), bf16[64,4,4,256]{3,2,1,0:T(4,128)(2,1)S(1)}, u32[]{:S(2)}, u32[]{:S(2)}) async-start(bf16[64,4,4,256]{3,2,1,0:T(4,128)(2,1)} %copy.122), calls=%async_computation.5 | async-start | bytes 1048576 | tf_op jit(solution)/shard_map/all_to_all | solution.py:152
  157.3 19.8 %all-to-all-start.4 = ((bf16[64,4,4,256]{3,2,1,0:T(4,128)(2,1)}), bf16[64,4,4,256]{3,2,1,0:T(4,128)(2,1)S(1)}, u32[]{:S(2)}, u32[]{:S(2)}) async-start(bf16[64,4,4,256]{3,2,1,0:T(4,128)(2,1)} %copy.120), calls=%async_computation.4 | async-start | bytes 1048576 | tf_op jit(solution)/shard_map/all_to_all | solution.py:151
  178.5 16.7 %collective-permute-start = (bf16[1,2,16,4,256]{4,2,3,0,1:T(8,128)(2,1)S(1)}, bf16[1,2,16,4,256]{4,2,3,0,1:T(8,128)(2,1)S(1)}, u32[]{:S(2)}, u32[]{:S(2)}) collective-permute-start(bf16[1,2,16,4,256]{4,2,3,0,1:T(8,128)(2,1)S(1)} %get-tuple-element.13), channel_id=1, source_target_pairs={{0,1},{1,2},{2,3},{3,4},{4,5},{5,6},{6,7},{7,0},{8,9},{9,10},{10,1... | collective-permute-start | bytes 196616 | tf_op jit(solution)/shard_map/ppermute | solution.py:31
  183.9 13.3 %collective-permute-start.1 = (bf16[1,2,16,4,256]{4,2,3,0,1:T(8,128)(2,1)S(1)}, bf16[1,2,16,4,256]{4,2,3,0,1:T(8,128)(2,1)S(1)}, u32[]{:S(2)}, u32[]{:S(2)}) collective-permute-start(bf16[1,2,16,4,256]{4,2,3,0,1:T(8,128)(2,1)S(1)} %get-tuple-element.12), channel_id=1, source_target_pairs={{0,2},{1,3},{2,4},{3,5},{4,6},{5,7},{6,0},{7,1},{8,10},{9,11},{10,... | collective-permute-start | bytes 196616 | tf_op jit(solution)/shard_map/ppermute | solution.py:31
  185.0 12.8 %collective-permute-start.2 = (bf16[1,2,16,4,256]{4,2,3,0,1:T(8,128)(2,1)S(1)}, bf16[1,2,16,4,256]{4,2,3,0,1:T(8,128)(2,1)S(1)}, u32[]{:S(2)}, u32[]{:S(2)}) collective-permute-start(bf16[1,2,16,4,256]{4,2,3,0,1:T(8,128)(2,1)S(1)} %get-tuple-element.11), channel_id=1, source_target_pairs={{0,3},{1,4},{2,5},{3,6},{4,7},{5,0},{6,1},{7,2},{8,11},{9,12},{10,... | collective-permute-start | bytes 196616 | tf_op jit(solution)/shard_map/ppermute | solution.py:31
  186.0 11.8 %collective-permute-start.3 = (bf16[1,2,16,4,256]{4,2,3,0,1:T(8,128)(2,1)S(1)}, bf16[1,2,16,4,256]{4,2,3,0,1:T(8,128)(2,1)S(1)}, u32[]{:S(2)}, u32[]{:S(2)}) collective-permute-start(bf16[1,2,16,4,256]{4,2,3,0,1:T(8,128)(2,1)S(1)} %get-tuple-element.10), channel_id=1, source_target_pairs={{0,4},{1,5},{2,6},{3,7},{4,0},{5,1},{6,2},{7,3},{8,12},{9,13},{10,... | collective-permute-start | bytes 196616 | tf_op jit(solution)/shard_map/ppermute | solution.py:31
  187.5 10.4 %collective-permute-start.4 = (bf16[1,2,16,4,256]{4,2,3,0,1:T(8,128)(2,1)S(1)}, bf16[1,2,16,4,256]{4,2,3,0,1:T(8,128)(2,1)S(1)}, u32[]{:S(2)}, u32[]{:S(2)}) collective-permute-start(bf16[1,2,16,4,256]{4,2,3,0,1:T(8,128)(2,1)S(1)} %get-tuple-element.9), channel_id=1, source_target_pairs={{0,5},{1,6},{2,7},{3,0},{4,1},{5,2},{6,3},{7,4},{8,13},{9,14},{10,... | collective-permute-start | bytes 196616 | tf_op jit(solution)/shard_map/ppermute | solution.py:31
  191.8 13.0 %all-to-all-start.6 = ((bf16[2,128,4,256]{3,2,0,1:T(4,128)(2,1)}), bf16[2,128,4,256]{3,2,0,1:T(4,128)(2,1)S(1)}, u32[]{:S(2)}, u32[]{:S(2)}) async-start(bf16[2,128,4,256]{3,2,0,1:T(4,128)(2,1)} %copy.124), calls=%async_computation.6 | async-start | bytes 1048576 | tf_op jit(solution)/shard_map/all_to_all | solution.py:156
  195.3 8.7 %collective-permute-start.5 = (bf16[1,2,16,4,256]{4,2,3,0,1:T(8,128)(2,1)S(1)}, bf16[1,2,16,4,256]{4,2,3,0,1:T(8,128)(2,1)S(1)}, u32[]{:S(2)}, u32[]{:S(2)}) collective-permute-start(bf16[1,2,16,4,256]{4,2,3,0,1:T(8,128)(2,1)S(1)} %get-tuple-element.8), channel_id=1, source_target_pairs={{0,6},{1,7},{2,0},{3,1},{4,2},{5,3},{6,4},{7,5},{8,14},{9,15},{10,... | collective-permute-start | bytes 196616 | tf_op jit(solution)/shard_map/ppermute | solution.py:31
  197.1 7.7 %collective-permute-start.6 = (bf16[1,2,16,4,256]{4,2,3,0,1:T(8,128)(2,1)S(1)}, bf16[1,2,16,4,256]{4,2,3,0,1:T(8,128)(2,1)S(1)}, u32[]{:S(2)}, u32[]{:S(2)}) collective-permute-start(bf16[1,2,16,4,256]{4,2,3,0,1:T(8,128)(2,1)S(1)} %get-tuple-element.7), channel_id=1, source_target_pairs={{0,7},{1,0},{2,1},{3,2},{4,3},{5,4},{6,5},{7,6},{8,15},{9,8},{10,9... | collective-permute-start | bytes 196616 | tf_op jit(solution)/shard_map/ppermute | solution.py:31
